TPU v7x, 128 devices: a whole 4x4x4 slice. The times are simulated.
128 devices in a mesh: pts: 16 (over z, y_hi, core), grp: 8 (over x, y_lo).
Axes of the slice: x: 4, y: 4 (y_hi: 2, y_lo: 2; y = y_hi * 2 + y_lo), z: 4, core: 2. Of those that a mesh axis runs over, the one named last changes fastest.
Arguments:
- adjoint_in: bfloat16 [1152, 1280, 256], P(None, ('pts', 'grp')), may hold values from -6 to 6
- land_sea: int32 [1280, 256], P(('pts', 'grp')), may hold values 0 or 1
- depth_class: int32 [1280, 256], P(('pts', 'grp')), may hold values from 0 to 7
- damping: float32 [1280, 256], P(('pts', 'grp')), may hold values from 0.05 to 0.5
- transparency: float32 [1280, 256], P(('pts', 'grp')), may hold values from 0.6 to 1
- outlets: int32 [64], replicated, may hold values from 0 to 327679
- flux_weight: float32 [1152], replicated, may hold values from 0.5 to 2
- jacobian: bfloat16 [1152, 1152], replicated, may hold values from -0.1875 to 0.1875
- source_scale: float32 [8], replicated, may hold values from 0.1 to 0.5
- freq_damp: float32 [1152], replicated, may hold values from 0.2 to 1
- courant: float32 [32], replicated, may hold values from 0.3 to 0.45
- wind_growth: float32 [1152], replicated, may hold values from 0.01 to 0.06
Outputs:
- adjoint_out: bfloat16 [1152, 1280, 256], P(None, ('pts', 'grp'))
- wind_sens: float32 [2, 1280, 256], P(None, ('pts', 'grp'))
All inputs are finite; a program needn't handle non-finite values. No bound on the sum of `land_sea` on one device may be relied on, other than what follows from the above.
Results may differ from a plain program's by a relative error of at most 0.0057.
Values may be sent and summed in bfloat16 or wider, within the bound.
No kernel may reach another device: no remote copies, remote signals or barrier semaphores. Data moves between devices by JAX's collectives and lax.ppermute only.
A program may use at most 128 MiB of HBM per device.

v0:
```python
import math
import jax
import jax.numpy as jnp
from jax import lax
from jax.sharding import PartitionSpec as P

DIR = 36
FREQ = 32
NSUB = 4
NCLASS = 8


def direction_cosines():
    angles = 2.0 * math.pi * (jnp.arange(DIR, dtype=jnp.float32) + 0.5) / DIR
    return (jnp.tile(jnp.cos(angles), FREQ), jnp.tile(jnp.sin(angles), FREQ))


def upwind_weights(courant):
    cosine, sine = direction_cosines()
    speed = jnp.repeat(courant, DIR)
    along_x = speed * cosine
    along_y = speed * sine
    zeros = jnp.zeros_like(along_x)
    return (
        jnp.maximum(along_x, zeros),
        jnp.maximum(-along_x, zeros),
        jnp.maximum(along_y, zeros),
        jnp.maximum(-along_y, zeros),
        1.0 - jnp.abs(along_x) - jnp.abs(along_y),
    )


def propagate(spectrum, weights, passage):
    eastward, westward, northward, southward, centre_keep = tuple(
        (piece[:, None, None] for piece in weights)
    )
    for substep in range(NSUB):
        padded = jnp.pad(spectrum, ((0, 0), (1, 1), (1, 1)))
        spectrum = passage * (
            centre_keep * spectrum
            + eastward * padded[:, 1:-1, 2:]
            + westward * padded[:, 1:-1, :-2]
            + northward * padded[:, 2:, 1:-1]
            + southward * padded[:, :-2, 1:-1]
        )
    return spectrum


def source_adjoint(spectrum, jacobian, source_rate, damp_rows, freq_damp):
    coupled = lax.dot_general(
        jacobian, spectrum, (((0,), (0,)), ((), ())), preferred_element_type=jnp.float32
    )
    values = spectrum.astype(jnp.float32)
    return (
        values + source_rate[None, :] * coupled - damp_rows[None, :] * freq_damp[:, None] * values
    ).astype(jnp.bfloat16)


def body(
    adjoint_in,
    land_sea,
    depth_class,
    damping,
    transparency,
    outlets,
    flux_weight,
    jacobian,
    source_scale,
    freq_damp,
    courant,
    wind_growth,
):
    components, row_count, lon_count = adjoint_in.shape
    devices = lax.axis_size(("pts", "grp"))
    per_device = components // devices
    point_count = row_count * lon_count
    position = lax.axis_index(("pts", "grp"))
    ocean_local = land_sea.astype(jnp.float32)
    passage_local = ocean_local * transparency
    coastline = lax.all_gather(passage_local, ("pts", "grp"), axis=0, tiled=True)
    cosine, sine = direction_cosines()
    forcing = jnp.stack([wind_growth * cosine, wind_growth * sine])
    ocean_rows = ocean_local.reshape(point_count)
    classes = depth_class.reshape(point_count)
    class_ids = jnp.arange(NCLASS, dtype=jnp.int32)[:, None]
    source_rate = jnp.sum(
        jnp.where(classes[None, :] == class_ids, source_scale[:, None], 0.0), axis=0
    )
    damp_rows = damping.reshape(point_count)
    flat_index = position * point_count + jnp.arange(point_count, dtype=jnp.int32)
    seed_count = jnp.sum((flat_index[None, :] == outlets[:, None]).astype(jnp.float32), axis=0)
    incoming = adjoint_in.reshape(components, point_count)
    seeded = (
        ocean_rows[None, :]
        * (incoming.astype(jnp.float32) + flux_weight[:, None] * seed_count[None, :])
    ).astype(jnp.bfloat16)
    mixed = source_adjoint(seeded, jacobian, source_rate, damp_rows, freq_damp)
    wind_first = jnp.dot(
        forcing, seeded, precision=lax.Precision.HIGHEST, preferred_element_type=jnp.float32
    )
    arrived = lax.all_to_all(
        mixed.reshape(components, row_count, lon_count),
        ("pts", "grp"),
        split_axis=0,
        concat_axis=1,
        tiled=True,
    )
    offset = position * per_device
    local_weights = tuple(
        (
            lax.dynamic_slice_in_dim(piece, offset, per_device, 0)
            for piece in upwind_weights(courant)
        )
    )
    propagated = propagate(arrived.astype(jnp.float32), local_weights, coastline).astype(
        jnp.bfloat16
    )
    home = lax.all_to_all(
        propagated, ("pts", "grp"), split_axis=1, concat_axis=0, tiled=True
    ).reshape(components, point_count)
    adjoint_out = source_adjoint(home, jacobian, source_rate, damp_rows, freq_damp).reshape(
        components, row_count, lon_count
    )
    wind_second = jnp.dot(
        forcing, home, precision=lax.Precision.HIGHEST, preferred_element_type=jnp.float32
    )
    wind_sens = (wind_first + wind_second).reshape(2, row_count, lon_count)
    return (adjoint_out, wind_sens)


def solution(mesh):
    placed = (
        P(None, ("pts", "grp"), None),
        P(("pts", "grp"), None),
        P(("pts", "grp"), None),
        P(("pts", "grp"), None),
        P(("pts", "grp"), None),
        P(),
        P(),
        P(),
        P(),
        P(),
        P(),
        P(),
    )
    return jax.shard_map(
        body,
        mesh=mesh,
        in_specs=placed,
        out_specs=(P(None, ("pts", "grp"), None), P(None, ("pts", "grp"), None)),
        check_vma=False,
    )
```

profile of v0, /device:TPU:2, one launch (start us, length us, event | category | flops | bytes accessed | tf_op | source)
XLA Modules:
  0.0 821.9 jit_solution(16402472275892524580)
XLA Ops:
  9.5 9.9 %copy.44 = f32[1152,10,256]{0,2,1:T(8,128)} copy(bf16[1152,10,256]{2,0,1:T(8,128)(2,1)} %param.12) | data formatting | bytes 17694720 | tf_op jit(solution)/shard_map/convert_element_type | solution.py:95
  19.7 5.8 fusion.42
  25.6 10.9 %fusion.44 = bf16[1152,2560]{0,1:T(8,128)(2,1)} fusion(bf16[1152,2560]{0,1:T(8,128)(2,1)S(1)} %fusion.42, bf16[1152,1152]{1,0:T(8,128)(2,1)S(1)} %copy-done, f32[1152]{0:T(1024)S(1)} %copy-done.10, f32[2560]{0:T(1024)S(1)} %mul.129, f32[2560]{0:T(1024)S(1)} %select_reduce_fusion), kind=kOutput, calls=%fused_computation.67 | convolution fusion | flops 6815416320 | bytes 14475776 | tf_op jit(solution)/shard_map/dot_general | solution.py:50
  36.4 12.0 %copy.45 = bf16[1152,10,256]{2,1,0:T(8,128)(2,1)} copy(bf16[1152,10,256]{0,2,1:T(8,128)(2,1)} %bitcast.49) | data formatting | bytes 11796480 | tf_op jit(solution)/shard_map/reshape | solution.py:102
  48.5 10.9 %all-to-all-start = ((bf16[1152,10,256]{2,1,0:T(8,128)(2,1)}), bf16[1152,10,256]{2,1,0:T(8,128)(2,1)}, u32[]{:S(2)}, u32[]{:S(2)}) async-start(bf16[1152,10,256]{2,1,0:T(8,128)(2,1)} %copy.45), calls=%async_computation | async-start | bytes 18874368 | tf_op jit(solution)/shard_map/all_to_all | solution.py:101
  61.1 365.3 %all-gather.3.cloned.1.call-done = f32[128,10,256]{2,1,0:T(8,128)} async-done(((f32[1,10,256]{2,1,0:T(8,128)}), f32[128,10,256]{2,1,0:T(8,128)}) %all-gather.3.cloned.1.call-update) | async-done | bytes 1310736 | tf_op jit(solution)/shard_map/all_gather | solution.py:80
  429.0 9.9 %copy_convert_fusion = f32[1152,10,256]{2,0,1:T(8,128)} fusion(bf16[1152,10,256]{2,1,0:T(8,128)(2,1)} %all-to-all-done), kind=kLoop, calls=%fused_computation.68 | loop fusion | flops 2949120 | bytes 17694720 | tf_op jit(solution)/shard_map/convert_element_type | solution.py:115
  438.8 15.4 %reshape.62 = f32[128,9,10,256]{3,1,0,2:T(8,128)} reshape(f32[1152,10,256]{2,0,1:T(8,128)} %copy_convert_fusion) | data formatting | bytes 23592960 | tf_op jit(solution)/shard_map/convert_element_type | solution.py:115
  454.2 19.6 %copy.47 = f32[9,128,10,256]{3,2,1,0:T(8,128)} copy(f32[9,128,10,256]{3,0,1,2:T(8,128)} %bitcast.43) | data formatting | bytes 23592960 | tf_op jit(solution)/shard_map/convert_element_type | solution.py:115
  473.8 16.4 %reshape.61 = f32[9,1280,256]{2,1,0:T(8,128)} reshape(f32[9,128,10,256]{3,2,1,0:T(8,128)} %copy.47) | data formatting | bytes 23592960 | tf_op jit(solution)/shard_map/convert_element_type | solution.py:115
  490.2 25.7 %fusion.9 = f32[9,1280,256]{2,1,0:T(8,128)} fusion(f32[9,1280,256]{2,1,0:T(8,128)} %reshape.61, f32[9]{0:T(128)S(1)} %get-tuple-element.20, f32[9]{0:T(128)S(1)} %get-tuple-element.19, f32[9]{0:T(128)S(1)} %get-tuple-element.17, f32[9]{0:T(128)S(1)} %get-tuple-element.18, f32[9]{0:T(128)S(1)} %get-tuple-element.16, f32[1280,256]{1,0:T(8,128)} %reshape.64), kind=kLoop, calls=%fused_computation.31 | loop fusion | flops 29491200 | bytes 24903860 | tf_op jit(solution)/shard_map/mul | solution.py:39
  515.9 25.3 %fusion.18 = f32[9,1280,256]{2,1,0:T(8,128)} fusion(f32[9,1280,256]{2,1,0:T(8,128)} %fusion.9, f32[9]{0:T(128)S(1)} %get-tuple-element.20, f32[9]{0:T(128)S(1)} %get-tuple-element.19, f32[9]{0:T(128)S(1)} %get-tuple-element.17, f32[9]{0:T(128)S(1)} %get-tuple-element.18, f32[9]{0:T(128)S(1)} %get-tuple-element.16, f32[1280,256]{1,0:T(8,128)S(1)} %copy-done.1), kind=kLoop, calls=%fused_computation.40 | loop fusion | flops 29491200 | bytes 24903860 | tf_op jit(solution)/shard_map/mul | solution.py:39
  541.2 25.3 %fusion.27 = f32[9,1280,256]{2,1,0:T(8,128)} fusion(f32[9,1280,256]{2,1,0:T(8,128)} %fusion.18, f32[9]{0:T(128)S(1)} %get-tuple-element.20, f32[9]{0:T(128)S(1)} %get-tuple-element.19, f32[9]{0:T(128)S(1)} %get-tuple-element.17, f32[9]{0:T(128)S(1)} %get-tuple-element.18, f32[9]{0:T(128)S(1)} %get-tuple-element.16, f32[1280,256]{1,0:T(8,128)S(1)} %copy-done.1), kind=kLoop, calls=%fused_computation.49 | loop fusion | flops 29491200 | bytes 24903860 | tf_op jit(solution)/shard_map/mul | solution.py:39
  566.6 34.8 %fusion.37 = bf16[9,1280,256]{2,1,0:T(8,128)(2,1)} fusion(f32[9,1280,256]{2,1,0:T(8,128)} %fusion.27, f32[9]{0:T(128)S(1)} %get-tuple-element.20, f32[9]{0:T(128)S(1)} %get-tuple-element.19, f32[9]{0:T(128)S(1)} %get-tuple-element.17, f32[9]{0:T(128)S(1)} %get-tuple-element.18, f32[9]{0:T(128)S(1)} %get-tuple-element.16, f32[1280,256]{1,0:T(8,128)S(1)} %copy-done.1), kind=kLoop, calls=%fused_computation.59 | loop fusion | flops 32440320 | bytes 19005620 | tf_op jit(solution)/shard_map/convert_element_type | solution.py:115
  601.4 9.5 %copy.48 = bf16[9,1280,256]{2,0,1:T(8,128)(2,1)} copy(bf16[9,1280,256]{2,1,0:T(8,128)(2,1)} %fusion.37) | data formatting | bytes 11796480 | tf_op jit(solution)/shard_map/convert_element_type | solution.py:115
  610.9 9.3 %all-to-all-start.1 = ((bf16[9,1280,256]{2,0,1:T(8,128)(2,1)}), bf16[9,1280,256]{2,0,1:T(8,128)(2,1)}, u32[]{:S(2)}, u32[]{:S(2)}) async-start(bf16[9,1280,256]{2,0,1:T(8,128)(2,1)} %copy.48), calls=%async_computation.1 | async-start | bytes 20971520 | tf_op jit(solution)/shard_map/all_to_all | solution.py:118
  620.2 7.3 fusion.45
  627.5 126.8 %all-to-all-done.1 = bf16[9,1280,256]{2,0,1:T(8,128)(2,1)} async-done(((bf16[9,1280,256]{2,0,1:T(8,128)(2,1)}), bf16[9,1280,256]{2,0,1:T(8,128)(2,1)}, u32[]{:S(2)}, u32[]{:S(2)}) %all-to-all-start.1) | async-done | bytes 5898272 | tf_op jit(solution)/shard_map/all_to_all | solution.py:118
  754.3 12.1 %copy.50 = bf16[128,9,10,256]{3,2,1,0:T(8,128)(2,1)} copy(bf16[128,9,10,256]{3,1,2,0:T(8,128)(2,1)} %bitcast.7) | data formatting | bytes 11796480 | tf_op jit(solution)/shard_map/all_to_all | solution.py:118
  766.4 10.2 %copy.56 = bf16[144,8,10,256]{3,1,2,0:T(8,128)(2,1)} copy(bf16[144,8,10,256]{3,2,1,0:T(8,128)(2,1)} %bitcast.47) | data formatting | bytes 11796480
  776.6 8.8 %copy.51 = bf16[1152,2560]{0,1:T(8,128)(2,1)} copy(bf16[1152,2560]{1,0:T(8,128)(2,1)} %bitcast.44) | data formatting | bytes 11796480 | tf_op jit(solution)/shard_map/reshape | solution.py:120
  785.5 5.7 convolution_add_fusion
  791.1 14.8 %fusion.43 = bf16[1152,2560]{0,1:T(8,128)(2,1)} fusion(bf16[1152,2560]{0,1:T(8,128)(2,1)} %copy.51, bf16[1152,2560]{1,0:T(8,128)(2,1)} %bitcast.46, bf16[1152,1152]{1,0:T(8,128)(2,1)S(1)} %copy-done, f32[1152]{0:T(1024)S(1)} %copy-done.10, f32[2560]{0:T(1024)S(1)} %mul.129, f32[2560]{0:T(1024)S(1)} %select_reduce_fusion), kind=kOutput, calls=%fused_computation.66 | convolution fusion | flops 6815416320 | bytes 20374016 | tf_op jit(solution)/shard_map/dot_general | solution.py:50
  806.0 8.9 %copy.52 = bf16[1152,10,256]{2,0,1:T(8,128)(2,1)} copy(bf16[1152,10,256]{0,2,1:T(8,128)(2,1)} %bitcast.48) | data formatting | bytes 11796480
  (46 shorter events, 6.7 us)
Async XLA Ops:
  7.2 18.4 %copy-start = (bf16[1152,1152]{1,0:T(8,128)(2,1)S(1)}, bf16[1152,1152]{1,0:T(8,128)(2,1)}, u32[]{:S(2)}) copy-start(bf16[1152,1152]{1,0:T(8,128)(2,1)} %param.19) | copy-start | bytes 7962628
  7.2 12.3 %copy-start.7 = (s32[64]{0:T(128)S(1)}, s32[64]{0:T(128)}, u32[]{:S(2)}) copy-start(s32[64]{0:T(128)} %param.17) | copy-start | bytes 772
  7.2 12.4 %copy-start.8 = (f32[8]{0:T(128)S(1)}, f32[8]{0:T(128)}, u32[]{:S(2)}) copy-start(f32[8]{0:T(128)} %param.20) | copy-start | bytes 100
  7.2 12.5 %copy-start.5 = (f32[1152]{0:T(1024)S(1)}, f32[1152]{0:T(1024)}, u32[]{:S(2)}) copy-start(f32[1152]{0:T(1024)} %param.18) | copy-start | bytes 13828
  19.4 6.1 copy-start.10
  25.6 10.9 %copy-start.2 = (bf16[1152,2560]{0,1:T(8,128)(2,1)}, bf16[1152,2560]{0,1:T(8,128)(2,1)S(1)}, u32[]{:S(2)}) copy-start(bf16[1152,2560]{0,1:T(8,128)(2,1)S(1)} %fusion.42) | copy-start | bytes 17694724
  48.5 11.4 %copy-start.3 = (s32[10,256]{1,0:T(8,128)S(1)}, s32[10,256]{1,0:T(8,128)}, u32[]{:S(2)}) copy-start(s32[10,256]{1,0:T(8,128)} %param.13) | copy-start | bytes 30724
  48.5 11.4 %copy-start.4 = (f32[10,256]{1,0:T(8,128)S(1)}, f32[10,256]{1,0:T(8,128)}, u32[]{:S(2)}) copy-start(f32[10,256]{1,0:T(8,128)} %param.16) | copy-start | bytes 30724
  48.5 12.4 %copy-start.9 = (f32[32]{0:T(128)S(1)}, f32[32]{0:T(128)}, u32[]{:S(2)}) copy-start(f32[32]{0:T(128)} %param.22) | copy-start | bytes 388
  48.5 12.5 %copy-start.6 = (f32[1152]{0:T(1024)S(1)}, f32[1152]{0:T(1024)}, u32[]{:S(2)}) copy-start(f32[1152]{0:T(1024)} %param.23) | copy-start | bytes 13828
  48.5 380.5 %all-to-all-start = ((bf16[1152,10,256]{2,1,0:T(8,128)(2,1)}), bf16[1152,10,256]{2,1,0:T(8,128)(2,1)}, u32[]{:S(2)}, u32[]{:S(2)}) async-start(bf16[1152,10,256]{2,1,0:T(8,128)(2,1)} %copy.45), calls=%async_computation | async-start | bytes 18874368 | tf_op jit(solution)/shard_map/all_to_all | solution.py:101
  59.4 367.0 %all-gather.3.cloned.1.call-start = ((), (), s32[]{:S(2)}) async-start(), calls=%async_computation.2 | async-start | bytes 2113536 | tf_op jit(solution)/shard_map/all_gather | solution.py:80
  490.2 25.7 %copy-start.1 = (f32[1280,256]{1,0:T(8,128)S(1)}, f32[1280,256]{1,0:T(8,128)}, u32[]{:S(2)}) copy-start(f32[1280,256]{1,0:T(8,128)} %reshape.64) | copy-start | bytes 3932164
  610.9 143.4 %all-to-all-start.1 = ((bf16[9,1280,256]{2,0,1:T(8,128)(2,1)}), bf16[9,1280,256]{2,0,1:T(8,128)(2,1)}, u32[]{:S(2)}, u32[]{:S(2)}) async-start(bf16[9,1280,256]{2,0,1:T(8,128)(2,1)} %copy.48), calls=%async_computation.1 | async-start | bytes 20971520 | tf_op jit(solution)/shard_map/all_to_all | solution.py:118
Sparse Core Ops, SparseCore 0:
  62.5 363.9 all-gather.2
where the time goes:
time: 828 us; the launch traced here: 822 us
  waiting for transfers between devices  492 us (59%)
  other arithmetic  129 us (16%)
  local copies, waits for them, and re-layouts  127 us (15%)
  matrix products  38.7 us (5%)
  starting transfers between devices  20.6 us (2%)
  between operations  14.5 us (2%)
    all_gather x1, waiting for transfers between devices, body(): lax.all_gather(passage_local, ('pts', 'grp'), axis=0, tiled=True)  365 us
    all_to_all x1, waiting for transfers between devices, body(): lax.all_to_all(propagated, ('pts', 'grp'), split_axis=1, concat_axis=0, t...  127 us
    mul x3, other arithmetic, propagate(): passage * (centre_keep * spectrum + eastward * padded[:, 1:-1, 2:] + west...  76.3 us
    convert_element_type x3, local copies, waits for them, and re-layouts, body(): arrived.astype(jnp.float32)  51.4 us
    convert_element_type x1, other arithmetic, body(): propagate(arrived.astype(jnp.float32), local_weights, coastline)  34.8 us
    dot_general x2, matrix products, source_adjoint(): lax.dot_general(jacobian, spectrum, (((0,), (0,)), ((), ())), preferred_e...  25.7 us
    unnamed x25, local copies, waits for them, and re-layouts  21.6 us
  transfers between devices with their start and end apart: 3, of which 2 were waited for; matrix products, arithmetic and copies ran while one was open for 1% of the time, Pallas kernels for 0%

commit v1 on v0

--- a/solution.py
+++ b/solution.py
@@ -77,7 +77,12 @@
     position = lax.axis_index(("pts", "grp"))
     ocean_local = land_sea.astype(jnp.float32)
     passage_local = ocean_local * transparency
-    coastline = lax.all_gather(passage_local, ("pts", "grp"), axis=0, tiled=True)
+    coastline = jnp.concatenate(
+        lax.all_to_all(
+            jnp.stack([passage_local] * lax.axis_size(("pts", "grp"))), ("pts", "grp"), 0, 0
+        ),
+        axis=0,
+    )
     cosine, sine = direction_cosines()
     forcing = jnp.stack([wind_growth * cosine, wind_growth * sine])
     ocean_rows = ocean_local.reshape(point_count)

time: 828 us -> 576 us (0.70)
  waiting for transfers between devices: 492 us -> 243 us
  between operations: 14.5 us -> 1.05 us
    all_gather x1 -> x0, waiting for transfers between devices: 365 us -> none  [body(): lax.all_gather(passage_local, ('pts', 'grp'), axis=0, tiled=True)]
    all_to_all x1, waiting for transfers between devices: 0.01 us -> 116 us  [body(): lax.all_to_all(mixed.reshape(components, row_count, lon_count), ('pts', '...]
    all_to_all x0 -> x1, starting transfers between devices: none -> 11 us  [body(): lax.all_to_all(jnp.stack([passage_local] * lax.axis_size(('pts', 'grp')))...]
    unnamed x25 -> x20, local copies, waits for them, and re-layouts: 21.6 us -> 19.1 us
  transfers between devices with their start and end apart: 3 -> 3, of which waited for: 2 -> 2; matrix products, arithmetic and copies ran while one was open for 1% -> 9% of each run, Pallas kernels for 0% -> 0%
where the time goes in v1:
time: 576 us; the launch traced here: 569 us
  waiting for transfers between devices  243 us (42%)
  local copies, waits for them, and re-layouts  129 us (22%)
  other arithmetic  129 us (22%)
  matrix products  38.7 us (7%)
  starting transfers between devices  28.1 us (5%)
    all_to_all x1, waiting for transfers between devices, body(): lax.all_to_all(propagated, ('pts', 'grp'), split_axis=1, concat_axis=0, t...  127 us
    all_to_all x1, waiting for transfers between devices, body(): lax.all_to_all(mixed.reshape(components, row_count, lon_count), ('pts', '...  116 us
    mul x3, other arithmetic, propagate(): passage * (centre_keep * spectrum + eastward * padded[:, 1:-1, 2:] + west...  76.2 us
    convert_element_type x3, local copies, waits for them, and re-layouts, body(): arrived.astype(jnp.float32)  51.4 us
    convert_element_type x1, other arithmetic, body(): propagate(arrived.astype(jnp.float32), local_weights, coastline)  34.8 us
    dot_general x2, matrix products, source_adjoint(): lax.dot_general(jacobian, spectrum, (((0,), (0,)), ((), ())), preferred_e...  25.7 us
    unnamed x20, local copies, waits for them, and re-layouts  19.1 us
    all_to_all x1, local copies, waits for them, and re-layouts, body(): lax.all_to_all(propagated, ('pts', 'grp'), split_axis=1, concat_axis=0, t...  12.1 us
  transfers between devices with their start and end apart: 3, of which 2 were waited for; matrix products, arithmetic and copies ran while one was open for 9% of the time, Pallas kernels for 0%

profile of v1, /device:TPU:2, one launch (start us, length us, event | category | flops | bytes accessed | tf_op | source)
XLA Modules:
  0.0 568.7 jit_solution(18182555580563825384)
XLA Ops:
  3.1 11.0 %all-to-all-start = ((f32[128,10,256]{2,1,0:T(8,128)}), f32[128,10,256]{2,1,0:T(8,128)}, u32[]{:S(2)}, u32[]{:S(2)}) async-start(f32[128,10,256]{2,1,0:T(8,128)} %stack.8), calls=%async_computation | async-start | bytes 4194304 | tf_op jit(solution)/shard_map/all_to_all | solution.py:81
  16.3 9.9 %copy.44 = f32[1152,10,256]{0,2,1:T(8,128)} copy(bf16[1152,10,256]{2,0,1:T(8,128)(2,1)} %param.12) | data formatting | bytes 17694720 | tf_op jit(solution)/shard_map/convert_element_type | solution.py:100
  26.5 5.8 %fusion.42 = bf16[1152,2560]{0,1:T(8,128)(2,1)S(1)} fusion(f32[1152,10,256]{0,2,1:T(8,128)} %copy.44, f32[2560]{0:T(1024)S(1)} %convert_reduce_fusion, f32[1152]{0:T(1024)S(1)} %copy-done.3, f32[2560]{0:T(1024)S(1)} %mul.122), kind=kLoop, calls=%fused_computation.65 | loop fusion | flops 11796480 | bytes 17719808 | tf_op jit(solution)/shard_map/convert_element_type | solution.py:101
  32.3 10.9 %fusion.44 = bf16[1152,2560]{0,1:T(8,128)(2,1)} fusion(bf16[1152,2560]{0,1:T(8,128)(2,1)S(1)} %fusion.42, bf16[1152,1152]{1,0:T(8,128)(2,1)S(1)} %copy-done, f32[1152]{0:T(1024)S(1)} %copy-done.8, f32[2560]{0:T(1024)S(1)} %mul.132, f32[2560]{0:T(1024)S(1)} %select_reduce_fusion), kind=kOutput, calls=%fused_computation.67 | convolution fusion | flops 6815416320 | bytes 14475776 | tf_op jit(solution)/shard_map/dot_general | solution.py:50
  43.2 12.0 %copy.45 = bf16[1152,10,256]{2,1,0:T(8,128)(2,1)} copy(bf16[1152,10,256]{0,2,1:T(8,128)(2,1)} %bitcast.47) | data formatting | bytes 11796480 | tf_op jit(solution)/shard_map/reshape | solution.py:107
  55.2 10.7 %all-to-all-start.1 = ((bf16[1152,10,256]{2,1,0:T(8,128)(2,1)}), bf16[1152,10,256]{2,1,0:T(8,128)(2,1)}, u32[]{:S(2)}, u32[]{:S(2)}) async-start(bf16[1152,10,256]{2,1,0:T(8,128)(2,1)} %copy.45), calls=%async_computation.1 | async-start | bytes 18874368 | tf_op jit(solution)/shard_map/all_to_all | solution.py:106
  69.1 116.5 %all-to-all-done.1 = bf16[1152,10,256]{2,1,0:T(8,128)(2,1)} async-done(((bf16[1152,10,256]{2,1,0:T(8,128)(2,1)}), bf16[1152,10,256]{2,1,0:T(8,128)(2,1)}, u32[]{:S(2)}, u32[]{:S(2)}) %all-to-all-start.1) | async-done | bytes 5898272 | tf_op jit(solution)/shard_map/all_to_all | solution.py:106
  185.5 9.9 %copy_convert_fusion = f32[1152,10,256]{2,0,1:T(8,128)} fusion(bf16[1152,10,256]{2,1,0:T(8,128)(2,1)} %all-to-all-done.1), kind=kLoop, calls=%fused_computation.68 | loop fusion | flops 2949120 | bytes 17694720 | tf_op jit(solution)/shard_map/convert_element_type | solution.py:120
  195.4 15.4 %reshape.64 = f32[128,9,10,256]{3,1,0,2:T(8,128)} reshape(f32[1152,10,256]{2,0,1:T(8,128)} %copy_convert_fusion) | data formatting | bytes 23592960 | tf_op jit(solution)/shard_map/convert_element_type | solution.py:120
  210.8 19.6 %copy.47 = f32[9,128,10,256]{3,2,1,0:T(8,128)} copy(f32[9,128,10,256]{3,0,1,2:T(8,128)} %bitcast.41) | data formatting | bytes 23592960 | tf_op jit(solution)/shard_map/convert_element_type | solution.py:120
  230.4 16.4 %reshape.63 = f32[9,1280,256]{2,1,0:T(8,128)} reshape(f32[9,128,10,256]{3,2,1,0:T(8,128)} %copy.47) | data formatting | bytes 23592960 | tf_op jit(solution)/shard_map/convert_element_type | solution.py:120
  246.8 25.7 %fusion.9 = f32[9,1280,256]{2,1,0:T(8,128)} fusion(f32[9,1280,256]{2,1,0:T(8,128)} %reshape.63, f32[9]{0:T(128)S(1)} %get-tuple-element.20, f32[9]{0:T(128)S(1)} %get-tuple-element.19, f32[9]{0:T(128)S(1)} %get-tuple-element.17, f32[9]{0:T(128)S(1)} %get-tuple-element.18, f32[9]{0:T(128)S(1)} %get-tuple-element.16, f32[1280,256]{1,0:T(8,128)} %mul.115), kind=kLoop, calls=%fused_computation.31 | loop fusion | flops 29491200 | bytes 24903860 | tf_op jit(solution)/shard_map/mul | solution.py:39
  272.5 25.3 %fusion.18 = f32[9,1280,256]{2,1,0:T(8,128)} fusion(f32[9,1280,256]{2,1,0:T(8,128)} %fusion.9, f32[9]{0:T(128)S(1)} %get-tuple-element.20, f32[9]{0:T(128)S(1)} %get-tuple-element.19, f32[9]{0:T(128)S(1)} %get-tuple-element.17, f32[9]{0:T(128)S(1)} %get-tuple-element.18, f32[9]{0:T(128)S(1)} %get-tuple-element.16, f32[1280,256]{1,0:T(8,128)S(1)} %copy-done.1), kind=kLoop, calls=%fused_computation.40 | loop fusion | flops 29491200 | bytes 24903860 | tf_op jit(solution)/shard_map/mul | solution.py:39
  297.7 25.3 %fusion.27 = f32[9,1280,256]{2,1,0:T(8,128)} fusion(f32[9,1280,256]{2,1,0:T(8,128)} %fusion.18, f32[9]{0:T(128)S(1)} %get-tuple-element.20, f32[9]{0:T(128)S(1)} %get-tuple-element.19, f32[9]{0:T(128)S(1)} %get-tuple-element.17, f32[9]{0:T(128)S(1)} %get-tuple-element.18, f32[9]{0:T(128)S(1)} %get-tuple-element.16, f32[1280,256]{1,0:T(8,128)S(1)} %copy-done.1), kind=kLoop, calls=%fused_computation.49 | loop fusion | flops 29491200 | bytes 24903860 | tf_op jit(solution)/shard_map/mul | solution.py:39
  323.0 34.8 %fusion.37 = bf16[9,1280,256]{2,1,0:T(8,128)(2,1)} fusion(f32[9,1280,256]{2,1,0:T(8,128)} %fusion.27, f32[9]{0:T(128)S(1)} %get-tuple-element.20, f32[9]{0:T(128)S(1)} %get-tuple-element.19, f32[9]{0:T(128)S(1)} %get-tuple-element.17, f32[9]{0:T(128)S(1)} %get-tuple-element.18, f32[9]{0:T(128)S(1)} %get-tuple-element.16, f32[1280,256]{1,0:T(8,128)S(1)} %copy-done.1), kind=kLoop, calls=%fused_computation.59 | loop fusion | flops 32440320 | bytes 19005620 | tf_op jit(solution)/shard_map/convert_element_type | solution.py:120
  357.8 9.5 %copy.48 = bf16[9,1280,256]{2,0,1:T(8,128)(2,1)} copy(bf16[9,1280,256]{2,1,0:T(8,128)(2,1)} %fusion.37) | data formatting | bytes 11796480 | tf_op jit(solution)/shard_map/convert_element_type | solution.py:120
  367.4 6.4 %all-to-all-start.2 = ((bf16[9,1280,256]{2,0,1:T(8,128)(2,1)}), bf16[9,1280,256]{2,0,1:T(8,128)(2,1)}, u32[]{:S(2)}, u32[]{:S(2)}) async-start(bf16[9,1280,256]{2,0,1:T(8,128)(2,1)} %copy.48), calls=%async_computation.2 | async-start | bytes 20971520 | tf_op jit(solution)/shard_map/all_to_all | solution.py:123
  373.8 7.3 %fusion.45 = f32[2,2560]{1,0:T(2,128)S(1)} fusion(bf16[1152,2560]{0,1:T(8,128)(2,1)} %copy-done.2, f32[1,1152]{1,0:T(1,128)S(1)} %stack.10, f32[1,1152]{1,0:T(1,128)S(1)} %stack.9), kind=kOutput, calls=%fused_computation.75 | convolution fusion | flops 70781184 | bytes 5927936 | tf_op jit(solution)/shard_map/dot_general | solution.py:103
  381.1 126.8 %all-to-all-done.2 = bf16[9,1280,256]{2,0,1:T(8,128)(2,1)} async-done(((bf16[9,1280,256]{2,0,1:T(8,128)(2,1)}), bf16[9,1280,256]{2,0,1:T(8,128)(2,1)}, u32[]{:S(2)}, u32[]{:S(2)}) %all-to-all-start.2) | async-done | bytes 5898272 | tf_op jit(solution)/shard_map/all_to_all | solution.py:123
  507.9 12.1 %copy.50 = bf16[128,9,10,256]{3,2,1,0:T(8,128)(2,1)} copy(bf16[128,9,10,256]{3,1,2,0:T(8,128)(2,1)} %bitcast.6) | data formatting | bytes 11796480 | tf_op jit(solution)/shard_map/all_to_all | solution.py:123
  520.0 10.2 %copy.56 = bf16[144,8,10,256]{3,1,2,0:T(8,128)(2,1)} copy(bf16[144,8,10,256]{3,2,1,0:T(8,128)(2,1)} %bitcast.45) | data formatting | bytes 11796480
  530.2 8.9 %copy.51 = bf16[1152,2560]{0,1:T(8,128)(2,1)} copy(bf16[1152,2560]{1,0:T(8,128)(2,1)} %bitcast.42) | data formatting | bytes 11796480 | tf_op jit(solution)/shard_map/reshape | solution.py:125
  544.7 14.8 %fusion.43 = bf16[1152,2560]{0,1:T(8,128)(2,1)} fusion(bf16[1152,2560]{0,1:T(8,128)(2,1)} %copy.51, bf16[1152,2560]{1,0:T(8,128)(2,1)} %bitcast.44, bf16[1152,1152]{1,0:T(8,128)(2,1)S(1)} %copy-done, f32[1152]{0:T(1024)S(1)} %copy-done.8, f32[2560]{0:T(1024)S(1)} %mul.132, f32[2560]{0:T(1024)S(1)} %select_reduce_fusion), kind=kOutput, calls=%fused_computation.66 | convolution fusion | flops 6815416320 | bytes 20374016 | tf_op jit(solution)/shard_map/dot_general | solution.py:50
  559.6 8.9 %copy.52 = bf16[1152,10,256]{2,0,1:T(8,128)(2,1)} copy(bf16[1152,10,256]{0,2,1:T(8,128)(2,1)} %bitcast.46) | data formatting | bytes 11796480
  (42 shorter events, 13.7 us)
Async XLA Ops:
  0.6 31.6 %copy-start = (bf16[1152,1152]{1,0:T(8,128)(2,1)S(1)}, bf16[1152,1152]{1,0:T(8,128)(2,1)}, u32[]{:S(2)}) copy-start(bf16[1152,1152]{1,0:T(8,128)(2,1)} %param.19) | copy-start | bytes 7962628
  1.5 24.6 %copy-start.5 = (s32[64]{0:T(128)S(1)}, s32[64]{0:T(128)}, u32[]{:S(2)}) copy-start(s32[64]{0:T(128)} %param.17) | copy-start | bytes 772
  1.5 24.8 %copy-start.6 = (f32[8]{0:T(128)S(1)}, f32[8]{0:T(128)}, u32[]{:S(2)}) copy-start(f32[8]{0:T(128)} %param.20) | copy-start | bytes 100
  1.5 24.9 %copy-start.3 = (f32[1152]{0:T(1024)S(1)}, f32[1152]{0:T(1024)}, u32[]{:S(2)}) copy-start(f32[1152]{0:T(1024)} %param.18) | copy-start | bytes 13828
  3.1 52.1 %all-to-all-start = ((f32[128,10,256]{2,1,0:T(8,128)}), f32[128,10,256]{2,1,0:T(8,128)}, u32[]{:S(2)}, u32[]{:S(2)}) async-start(f32[128,10,256]{2,1,0:T(8,128)} %stack.8), calls=%async_computation | async-start | bytes 4194304 | tf_op jit(solution)/shard_map/all_to_all | solution.py:81
  26.2 6.1 %copy-start.8 = (f32[1152]{0:T(1024)S(1)}, f32[1152]{0:T(1024)}, u32[]{:S(2)}) copy-start(f32[1152]{0:T(1024)} %param.21) | copy-start | bytes 13828
  32.3 10.9 %copy-start.2 = (bf16[1152,2560]{0,1:T(8,128)(2,1)}, bf16[1152,2560]{0,1:T(8,128)(2,1)S(1)}, u32[]{:S(2)}) copy-start(bf16[1152,2560]{0,1:T(8,128)(2,1)S(1)} %fusion.42) | copy-start | bytes 17694724
  55.2 11.1 %copy-start.7 = (f32[32]{0:T(128)S(1)}, f32[32]{0:T(128)}, u32[]{:S(2)}) copy-start(f32[32]{0:T(128)} %param.22) | copy-start | bytes 388
  55.2 11.3 %copy-start.4 = (f32[1152]{0:T(1024)S(1)}, f32[1152]{0:T(1024)}, u32[]{:S(2)}) copy-start(f32[1152]{0:T(1024)} %param.23) | copy-start | bytes 13828
  55.2 130.3 %all-to-all-start.1 = ((bf16[1152,10,256]{2,1,0:T(8,128)(2,1)}), bf16[1152,10,256]{2,1,0:T(8,128)(2,1)}, u32[]{:S(2)}, u32[]{:S(2)}) async-start(bf16[1152,10,256]{2,1,0:T(8,128)(2,1)} %copy.45), calls=%async_computation.1 | async-start | bytes 18874368 | tf_op jit(solution)/shard_map/all_to_all | solution.py:106
  246.8 25.7 %copy-start.1 = (f32[1280,256]{1,0:T(8,128)S(1)}, f32[1280,256]{1,0:T(8,128)}, u32[]{:S(2)}) copy-start(f32[1280,256]{1,0:T(8,128)} %mul.115) | copy-start | bytes 3932164
  367.4 140.5 %all-to-all-start.2 = ((bf16[9,1280,256]{2,0,1:T(8,128)(2,1)}), bf16[9,1280,256]{2,0,1:T(8,128)(2,1)}, u32[]{:S(2)}, u32[]{:S(2)}) async-start(bf16[9,1280,256]{2,0,1:T(8,128)(2,1)} %copy.48), calls=%async_computation.2 | async-start | bytes 20971520 | tf_op jit(solution)/shard_map/all_to_all | solution.py:123
